TPU v7x, 32 devices: a whole 2x2x4 slice. The times are simulated.
32 devices in a mesh: section: 4 (over z), sector: 4 (over y, core), comp: 2 (over x).
Axes of the slice: x: 2, y: 2, z: 4, core: 2. Of those that a mesh axis runs over, the one named last changes fastest.
Arguments:
- env_in: bfloat16 [2, 8, 4, 512, 128], P('comp', None, 'sector', 'section'), may hold values from -6 to 6
- site_tensor: bfloat16 [3, 4, 512, 4, 512], P(None, 'sector', None, None, 'section'), may hold values from -0.125 to 0.125
- bra_tensor: bfloat16 [3, 4, 128, 4, 128], P(None, 'sector'), may hold values from -0.5 to 0.5
- mixing: float32 [3, 4, 8, 8], replicated, may hold values from -2 to 2
- sector_sizes: int32 [4, 4], replicated, may hold values from 256 to 512, as said below
- targets: int32 [3, 4, 4], replicated, may hold values from 0 to 3, as said below
Outputs:
- env_out: bfloat16 [3, 2, 8, 4, 512, 128], P(None, 'comp', None, 'sector', 'section')
- total_env: bfloat16 [8, 4, 512, 128], P('comp', 'sector', 'section')
Inputs may be any that keep to these rules, and one draw needn't show every extreme that they name: `sector_sizes`: on every bond some sector has exactly 512 states. For each site and source sector a the 4 targets are distinct and differ from a by at most 3; at every site some target lies 3 above its source sector and some 3 below.
All inputs are finite; a program needn't handle non-finite values.
Results may differ from a plain program's by a relative error of at most 0.02.
Values may be sent and summed in bfloat16 or wider, within the bound.
A program may use at most 64 MiB of HBM per device.

v0:
```python
import jax
import jax.numpy as jnp
from jax import lax
from jax.sharding import PartitionSpec as P


def local(env_in, site_tensor, bra_tensor, mixing, sector_sizes, targets):
    section_index = lax.axis_index("section")
    sector_index = lax.axis_index("sector")
    sector_count = lax.axis_size("sector")
    site_count = site_tensor.shape[0]
    full_rows = site_tensor.shape[2]
    local_rows = site_tensor.shape[4]
    row_ids = jnp.arange(full_rows, dtype=jnp.int32)
    own_rows = section_index * local_rows + jnp.arange(local_rows, dtype=jnp.int32)
    keep_first = (own_rows < sector_sizes[0, sector_index]).astype(jnp.bfloat16)
    current = env_in[:, :, 0] * keep_first[None, None, :, None]
    results = []
    for site_index in range(site_count):
        targets_row = targets[site_index, sector_index]
        size_out = sector_sizes[site_index + 1][targets_row]
        keep_in = (row_ids < sector_sizes[site_index, sector_index]).astype(jnp.bfloat16)
        keep_out = (own_rows[None, :] < size_out[:, None]).astype(jnp.bfloat16)
        masked = site_tensor[site_index, 0] * keep_in[:, None, None] * keep_out[None, :, :]
        weights = mixing[site_index]
        mixed_rows = jnp.einsum(
            "sdc,bcik->bdsik",
            weights,
            lax.all_gather(current, "section", axis=2, tiled=True).astype(jnp.float32),
            precision=lax.Precision.HIGHEST,
        ).astype(jnp.bfloat16)
        left_total = jnp.einsum(
            "iso,bdsik->bdsok", masked, mixed_rows, preferred_element_type=jnp.float32
        )
        left_part = left_total.astype(jnp.bfloat16)
        partial_value = jnp.einsum(
            "bdsok,ksl->bdsol",
            left_part,
            bra_tensor[site_index, 0],
            preferred_element_type=jnp.float32,
        ).astype(jnp.bfloat16)
        onehot = (
            targets_row[None, :] == jnp.arange(sector_count, dtype=jnp.int32)[:, None]
        ).astype(jnp.bfloat16)
        outgoing = jnp.einsum(
            "js,bdsol->jbdol", onehot, partial_value, preferred_element_type=jnp.float32
        ).astype(jnp.bfloat16)
        received = lax.all_to_all(outgoing, "sector", split_axis=0, concat_axis=0, tiled=True)
        updated = jnp.sum(received, axis=0, dtype=jnp.float32)
        current = updated.astype(jnp.bfloat16)
        results.append(current)
    stacked = jnp.stack(results)[:, :, :, None]
    batch_term = jnp.sum(current.astype(jnp.float32), axis=0)
    summed = lax.psum_scatter(
        batch_term.astype(jnp.bfloat16), "comp", scatter_dimension=0, tiled=True
    )
    return (stacked, summed[:, None])


def solution(mesh):
    in_specs = (
        P("comp", None, "sector", "section", None),
        P(None, "sector", None, None, "section"),
        P(None, "sector", None, None, None),
        P(),
        P(),
        P(),
    )
    out_specs = (
        P(None, "comp", None, "sector", "section", None),
        P("comp", "sector", "section", None),
    )
    return jax.shard_map(local, mesh=mesh, in_specs=in_specs, out_specs=out_specs, check_vma=False)
```

profile of v0, /device:TPU:0, one launch (start us, length us, event | category | flops | bytes accessed | tf_op | source)
XLA Modules:
  0.0 202.3 jit_solution(12540820073185199314)
XLA Ops:
  7.2 0.0 all-gather.6.cloned.1.call-start
  7.2 1.5 constant_dynamic-slice_fusion.4
  8.7 0.6 compare_convert_fusion.3
  9.3 1.9 bitcast_multiply_fusion.3
  11.2 0.0 all-gather.6.cloned.1.call-update
  11.2 0.0 all-gather.8.cloned.1.call-start
  11.3 0.8 slice_bitcast_fusion
  12.1 0.7 fusion.74
  12.8 0.6 gather_fusion.1
  13.4 0.6 gather_fusion.2
  14.1 0.6 gather_fusion
  14.7 0.6 fusion.62
  15.4 0.7 fusion.77
  16.1 1.3 fusion.65
  17.4 0.1 compare_convert_fusion
  17.5 1.2 fusion.78
  18.6 2.8 %fusion.45 = (bf16[512,4,128,1]{2,1,0,3:T(4,128)(2,1)S(1)}, bf16[512,4,128,1]{2,1,0,3:T(4,128)(2,1)S(1)}, bf16[512,4,128,1]{2,1,0,3:T(4,128)(2,1)S(1)}) fusion(bf16[3,1,512,4,128]{4,3,2,1,0:T(4,128)(2,1)S(1)} %copy-done, bf16[512]{0:T(512)(128)(2,1)S(1)} %get-tuple-element.32, bf16[4,128]{1,0:T(4,128)(2,1)S(1)} %get-tuple-element.26, ...), kind=kLoop, calls=%fused_computation.40 | loop fusion | flops 1572864 | bytes 3151872 | tf_op jit(solution)/shard_map/mul | solution.py:24
  21.5 20.5 %all-gather.6.cloned.1.call-done = bf16[1,8,512,128]{3,1,0,2:T(8,128)(2,1)} async-done(((bf16[1,8,128,128]{3,1,0,2:T(8,128)(2,1)}), bf16[1,8,512,128]{3,1,0,2:T(8,128)(2,1)}) %all-gather.6.cloned.1.call-update) | async-done | bytes 1048592 | tf_op jit(solution)/shard_map/all_gather | solution.py:29
  42.0 6.6 %convert_bitcast_fusion.2 = bf16[8,4,512,128]{3,0,1,2:T(8,128)(2,1)} fusion(bf16[1,8,512,128]{3,1,0,2:T(8,128)(2,1)} %all-gather.6.cloned.1.call-done, f32[3,4,8,8]{3,2,1,0:T(8,128)} %param.9), kind=kOutput, calls=%fused_computation.11 | convolution fusion | flops 203423744 | bytes 5259264 | tf_op jit(solution)/shard_map/sdc,bcik->bdsik/dot_general | solution.py:26
  48.6 4.4 %fusion.15 = bf16[8,4,128,128]{3,2,0,1:T(8,128)(2,1)S(1)} fusion(bf16[8,4,512,128]{3,0,1,2:T(8,128)(2,1)} %convert_bitcast_fusion.2, bf16[512,4,128,1]{2,1,0,3:T(4,128)(2,1)S(1)} %get-tuple-element.9, bf16[1,1,128,4,128]{4,3,2,1,0:T(4,128)(2,1)S(1)} %get-tuple-element.13), kind=kOutput, calls=%fused_computation.21 | convolution fusion | flops 672137216 | bytes 5898240 | tf_op jit(solution)/shard_map/bdsok,ksl->bdsol/dot_general | solution.py:36
  53.0 0.0 copy-start.1
  53.0 0.9 fusion.16
  53.9 0.2 copy.50
  54.2 17.0 %all_to_all.15 = bf16[4,1,8,128,128]{4,3,2,1,0:T(8,128)(2,1)S(1)} all-to-all(bf16[4,1,8,128,128]{4,3,2,1,0:T(8,128)(2,1)S(1)} %copy.50), channel_id=1, replica_groups=mesh['section'=4,'sector'=4,'comp'=2] {'sector'}, dimensions={0} | all-to-all | bytes 2097152 | tf_op jit(solution)/shard_map/all_to_all | solution.py:48
  71.2 0.2 reduce_sum.44
  71.4 0.9 copy.52
  72.3 0.0 all-gather.8.cloned.1.call-update
  72.3 0.2 all-gather.10.cloned.1.call-start
  72.5 26.4 %all-gather.8.cloned.1.call-done = bf16[8,512,128]{2,0,1:T(8,128)(2,1)} async-done(((bf16[8,128,128]{2,0,1:T(8,128)(2,1)}), bf16[8,512,128]{2,0,1:T(8,128)(2,1)}) %all-gather.8.cloned.1.call-update) | async-done | bytes 1048592 | tf_op jit(solution)/shard_map/all_gather | solution.py:29
  99.0 6.2 %convert_bitcast_fusion.1 = bf16[8,4,512,128]{3,0,1,2:T(8,128)(2,1)} fusion(bf16[8,512,128]{2,0,1:T(8,128)(2,1)} %all-gather.8.cloned.1.call-done, f32[3,4,8,8]{3,2,1,0:T(8,128)S(1)} %copy-done.1), kind=kOutput, calls=%fused_computation.10 | convolution fusion | flops 203423744 | bytes 5259264 | tf_op jit(solution)/shard_map/sdc,bcik->bdsik/dot_general | solution.py:26
  105.2 4.4 %fusion.17 = bf16[8,4,128,128]{3,2,0,1:T(8,128)(2,1)S(1)} fusion(bf16[8,4,512,128]{3,0,1,2:T(8,128)(2,1)} %convert_bitcast_fusion.1, bf16[512,4,128,1]{2,1,0,3:T(4,128)(2,1)S(1)} %get-tuple-element.10, bf16[1,1,128,4,128]{4,3,2,1,0:T(4,128)(2,1)S(1)} %get-tuple-element.12), kind=kOutput, calls=%fused_computation.23 | convolution fusion | flops 672137216 | bytes 5898240 | tf_op jit(solution)/shard_map/bdsok,ksl->bdsol/dot_general | solution.py:36
  109.6 0.9 fusion.18
  110.5 0.2 copy.58
  110.8 17.0 %all_to_all.16 = bf16[4,1,8,128,128]{4,3,2,1,0:T(8,128)(2,1)S(1)} all-to-all(bf16[4,1,8,128,128]{4,3,2,1,0:T(8,128)(2,1)S(1)} %copy.58), channel_id=1, replica_groups=mesh['section'=4,'sector'=4,'comp'=2] {'sector'}, dimensions={0} | all-to-all | bytes 2097152 | tf_op jit(solution)/shard_map/all_to_all | solution.py:48
  127.8 0.2 reduce_sum.46
  128.0 0.9 copy.60
  128.9 0.0 all-gather.10.cloned.1.call-update
  128.9 0.0 reduce-scatter.2.cloned.1.call-start
  129.0 26.6 %all-gather.10.cloned.1.call-done = bf16[8,512,128]{2,0,1:T(8,128)(2,1)} async-done(((bf16[8,128,128]{2,0,1:T(8,128)(2,1)}), bf16[8,512,128]{2,0,1:T(8,128)(2,1)}) %all-gather.10.cloned.1.call-update) | async-done | bytes 1048592 | tf_op jit(solution)/shard_map/all_gather | solution.py:29
  155.6 6.2 %convert_bitcast_fusion = bf16[8,4,512,128]{3,0,1,2:T(8,128)(2,1)} fusion(bf16[8,512,128]{2,0,1:T(8,128)(2,1)} %all-gather.10.cloned.1.call-done, f32[3,4,8,8]{3,2,1,0:T(8,128)S(1)} %copy-done.1), kind=kOutput, calls=%fused_computation.9 | convolution fusion | flops 203423744 | bytes 5259264 | tf_op jit(solution)/shard_map/sdc,bcik->bdsik/dot_general | solution.py:26
  161.8 4.4 %fusion.19 = bf16[8,4,128,128]{3,2,0,1:T(8,128)(2,1)S(1)} fusion(bf16[8,4,512,128]{3,0,1,2:T(8,128)(2,1)} %convert_bitcast_fusion, bf16[512,4,128,1]{2,1,0,3:T(4,128)(2,1)S(1)} %get-tuple-element.8, bf16[1,1,128,4,128]{4,3,2,1,0:T(4,128)(2,1)S(1)} %get-tuple-element.11), kind=kOutput, calls=%fused_computation.25 | convolution fusion | flops 672137216 | bytes 5898240 | tf_op jit(solution)/shard_map/bdsok,ksl->bdsol/dot_general | solution.py:36
  166.2 0.9 fusion.20
  167.1 0.2 copy.66
  167.4 17.0 %all_to_all.17 = bf16[4,1,8,128,128]{4,3,2,1,0:T(8,128)(2,1)S(1)} all-to-all(bf16[4,1,8,128,128]{4,3,2,1,0:T(8,128)(2,1)S(1)} %copy.66), channel_id=1, replica_groups=mesh['section'=4,'sector'=4,'comp'=2] {'sector'}, dimensions={0} | all-to-all | bytes 2097152 | tf_op jit(solution)/shard_map/all_to_all | solution.py:48
  184.4 0.9 reduce_sum.48
  185.3 0.0 reduce-scatter.2.cloned.1.call-update
  185.3 1.9 maximum_bitcast_fusion
  187.3 8.5 %reduce-scatter.2.cloned.1.call-done = bf16[4,128,128]{2,1,0:T(8,128)(2,1)} async-done(((bf16[8,128,128]{2,1,0:T(8,128)(2,1)}), bf16[4,128,128]{2,1,0:T(8,128)(2,1)}) %reduce-scatter.2.cloned.1.call-update) | async-done | bytes 131088 | tf_op jit(solution)/shard_map/reduce_scatter | solution.py:54
  (6 shorter events, 0.0 us)
Async XLA Ops:
  7.2 11.5 %copy-start = (bf16[3,1,512,4,128]{4,3,2,1,0:T(4,128)(2,1)S(1)}, bf16[3,1,512,4,128]{4,3,2,1,0:T(4,128)(2,1)}, u32[]{:S(2)}) copy-start(bf16[3,1,512,4,128]{4,3,2,1,0:T(4,128)(2,1)} %param.7) | copy-start | bytes 4718596
  7.2 34.8 %all-gather.6.cloned.1.call-start = ((), (), s32[]{:S(2)}) async-start(), calls=%async_computation.4 | async-start | bytes 1310720 | tf_op jit(solution)/shard_map/all_gather | solution.py:29
  11.2 87.8 %all-gather.8.cloned.1.call-start = ((), (), s32[]{:S(2)}) async-start(), calls=%async_computation.6 | async-start | bytes 1310720 | tf_op jit(solution)/shard_map/all_gather | solution.py:29
  53.0 46.0 %copy-start.1 = (f32[3,4,8,8]{3,2,1,0:T(8,128)S(1)}, f32[3,4,8,8]{3,2,1,0:T(8,128)}, u32[]{:S(2)}) copy-start(f32[3,4,8,8]{3,2,1,0:T(8,128)} %param.9) | copy-start | bytes 9220
  72.3 83.3 %all-gather.10.cloned.1.call-start = ((), (), s32[]{:S(2)}) async-start(), calls=%async_computation.7 | async-start | bytes 1310720 | tf_op jit(solution)/shard_map/all_gather | solution.py:29
  128.9 66.8 %reduce-scatter.2.cloned.1.call-start = ((), (), s32[]{:S(2)}) async-start(), calls=%async_computation.5 | async-start | bytes 393216 | tf_op jit(solution)/shard_map/reduce_scatter | solution.py:54
Sparse Core Ops, SparseCore 0:
  11.3 30.6 all-gather.5
  72.4 26.5 all-gather.7
  129.0 26.5 all-gather.9
  185.5 10.2 reduce-scatter.1
where the time goes:
time: 203 us; the launch traced here: 202 us
  waiting for transfers between devices  82.1 us (40%)
  blocking collectives  51 us (25%)
  matrix products  35 us (17%)
  between operations  13.9 us (7%)
  other arithmetic  11.3 us (6%)
  local copies, waits for them, and re-layouts  8.57 us (4%)
    all_gather x3, waiting for transfers between devices, local(): lax.all_gather(current, 'section', axis=2, tiled=True).astype(jnp.float32)  73.6 us
    all_to_all x3, blocking collectives, local(): lax.all_to_all(outgoing, 'sector', split_axis=0, concat_axis=0, tiled=True)  51 us
    dot_general x3, matrix products, local(): jnp.einsum('sdc,bcik->bdsik', weights, lax.all_gather(current, 'section',...  19.1 us
    dot_general x3, matrix products, local(): jnp.einsum('bdsok,ksl->bdsol', left_part, bra_tensor[site_index, 0], pref...  13.2 us
    reduce_scatter x1, waiting for transfers between devices, local(): lax.psum_scatter(batch_term.astype(jnp.bfloat16), 'comp', scatter_dimensi...  8.49 us
  transfers between devices with their start and end apart: 4, of which 4 were waited for; matrix products, arithmetic and copies ran while one was open for 6% of the time, Pallas kernels for 0%

commit v1 on v0

--- a/solution.py
+++ b/solution.py
@@ -2,6 +2,24 @@
 import jax.numpy as jnp
 from jax import lax
 from jax.sharding import PartitionSpec as P
+
+
+def ring_gather(array, axis, dim):
+    ways, here, step = (lax.axis_size(axis), lax.axis_index(axis), array.shape[dim])
+    shape = [n * ways if d == dim else n for d, n in enumerate(array.shape)]
+    full = lax.dynamic_update_slice_in_dim(
+        jnp.zeros(shape, array.dtype), array, here * step, axis=dim
+    )
+    going_up = going_down = array
+    for far in range(1, ways // 2 + 1):
+        going_up = lax.ppermute(going_up, axis, [(d, (d + 1) % ways) for d in range(ways)])
+        full = lax.dynamic_update_slice_in_dim(full, going_up, (here - far) % ways * step, axis=dim)
+        if 2 * far < ways:
+            going_down = lax.ppermute(going_down, axis, [(d, (d - 1) % ways) for d in range(ways)])
+            full = lax.dynamic_update_slice_in_dim(
+                full, going_down, (here + far) % ways * step, axis=dim
+            )
+    return full
 
 
 def local(env_in, site_tensor, bra_tensor, mixing, sector_sizes, targets):
@@ -26,7 +44,7 @@
         mixed_rows = jnp.einsum(
             "sdc,bcik->bdsik",
             weights,
-            lax.all_gather(current, "section", axis=2, tiled=True).astype(jnp.float32),
+            ring_gather(current, "section", 2).astype(jnp.float32),
             precision=lax.Precision.HIGHEST,
         ).astype(jnp.bfloat16)
         left_total = jnp.einsum(

time: 203 us -> 181 us (0.89)
  waiting for transfers between devices: 82.1 us -> 47 us
  starting transfers between devices: 0.34 us -> 12.9 us
  matrix products: 35 us -> 31.3 us
  local copies, waits for them, and re-layouts: 8.57 us -> 12.1 us
    all_gather x3 -> x0, waiting for transfers between devices: 73.6 us -> none  [local(): lax.all_gather(current, 'section', axis=2, tiled=True).astype(jnp.float32)]
    ppermute x0 -> x9, waiting for transfers between devices: none -> 39.9 us  [the longest x6 35.6 us: ring_gather(): lax.ppermute(going_up, axis, [(d, (d + 1) % ways) for d in range(ways)])]
    ppermute x0 -> x9, starting transfers between devices: none -> 12.8 us  [the longest x3 9.65 us: ring_gather(): lax.ppermute(going_down, axis, [(d, (d - 1) % ways) for d in range(ways)])]
    dynamic_update_slice x0 -> x12, local copies, waits for them, and re-layouts: none -> 4.19 us  [the longest x6 2.1 us: ring_gather(): lax.dynamic_update_slice_in_dim(full, going_up, (here - far) % ways * ste...]
    dot_general x3, matrix products: 19.1 us -> 15.4 us  [local(): jnp.einsum('sdc,bcik->bdsik', weights, ring_gather(current, 'section', 2)...]
  transfers between devices with their start and end apart: 4 -> 10, of which waited for: 4 -> 8; matrix products, arithmetic and copies ran while one was open for 6% -> 10% of each run, Pallas kernels for 0% -> 0%
where the time goes in v1:
time: 181 us
  blocking collectives  50.8 us (28%)
  waiting for transfers between devices  47 us (26%)
  matrix products  31.3 us (17%)
  between operations  14.3 us (8%)
  starting transfers between devices  12.9 us (7%)
  other arithmetic  12.2 us (7%)
  local copies, waits for them, and re-layouts  12.1 us (7%)
    all_to_all x3, blocking collectives, local(): lax.all_to_all(outgoing, 'sector', split_axis=0, concat_axis=0, tiled=True)  50.8 us
    ppermute x6, waiting for transfers between devices, ring_gather(): lax.ppermute(going_up, axis, [(d, (d + 1) % ways) for d in range(ways)])  35.6 us
    dot_general x3, matrix products, local(): jnp.einsum('sdc,bcik->bdsik', weights, ring_gather(current, 'section', 2)...  15.4 us
    dot_general x3, matrix products, local(): jnp.einsum('bdsok,ksl->bdsol', left_part, bra_tensor[site_index, 0], pref...  13.2 us
    ppermute x3, starting transfers between devices, ring_gather(): lax.ppermute(going_down, axis, [(d, (d - 1) % ways) for d in range(ways)])  9.65 us
    reduce_scatter x1, waiting for transfers between devices, local(): lax.psum_scatter(batch_term.astype(jnp.bfloat16), 'comp', scatter_dimensi...  7.15 us
    ppermute x3, waiting for transfers between devices, ring_gather(): lax.ppermute(going_down, axis, [(d, (d - 1) % ways) for d in range(ways)])  4.25 us
  transfers between devices with their start and end apart: 10, of which 8 were waited for; matrix products, arithmetic and copies ran while one was open for 10% of the time, Pallas kernels for 0%

profile of v1, /device:TPU:0, one launch (start us, length us, event | category | flops | bytes accessed | tf_op | source)
XLA Modules:
  0.0 180.6 jit_solution(7926887098573220511)
XLA Ops:
  7.2 1.5 constant_dynamic-slice_fusion.4
  8.7 0.6 compare_convert_fusion.3
  9.4 1.7 bitcast_multiply_fusion.3
  11.1 3.0 %collective-permute-start = (bf16[1,8,128,128]{3,2,1,0:T(8,128)(2,1)}, bf16[1,8,128,128]{3,2,1,0:T(8,128)(2,1)}, u32[]{:S(2)}, u32[]{:S(2)}) collective-permute-start(bf16[1,8,128,128]{3,2,1,0:T(8,128)(2,1)} %bitcast_multiply_fusion.3), channel_id=1, source_target_pairs={{0,8},{8,16},{16,24},{24,0},{1,9},{9,17},{17,25},{25,1},{2,10},{10... | collective-permute-start | bytes 786440 | tf_op jit(solution)/shard_map/ppermute | solution.py:15
  14.1 2.0 %collective-permute-start.1 = (bf16[1,8,128,128]{3,2,1,0:T(8,128)(2,1)}, bf16[1,8,128,128]{3,2,1,0:T(8,128)(2,1)}, u32[]{:S(2)}, u32[]{:S(2)}) collective-permute-start(bf16[1,8,128,128]{3,2,1,0:T(8,128)(2,1)} %bitcast_multiply_fusion.3), channel_id=1, source_target_pairs={{0,24},{8,0},{16,8},{24,16},{1,25},{9,1},{17,9},{25,17},{2,26},{10... | collective-permute-start | bytes 786440 | tf_op jit(solution)/shard_map/ppermute | solution.py:18
  16.2 1.0 bitcast_multiply_fusion.4
  17.2 0.8 slice_bitcast_fusion
  18.0 0.6 fusion.62
  18.7 0.7 fusion.74
  19.4 1.9 %fusion.78 = (bf16[1,1,128,4,128]{4,3,2,1,0:T(4,128)(2,1)S(1)}, bf16[1,1,128,4,128]{4,3,2,1,0:T(4,128)(2,1)}, bf16[1,1,128,4,128]{4,3,2,1,0:T(4,128)(2,1)}) fusion(bf16[3,1,128,4,128]{4,3,2,1,0:T(4,128)(2,1)} %param.8), kind=kLoop, calls=%fused_computation.113 | loop fusion | bytes 786432 | tf_op jit(solution)/shard_map/slice | solution.py:57
  21.3 0.6 gather_fusion.1
  21.9 0.6 gather_fusion.2
  22.5 0.6 gather_fusion
  23.2 1.2 fusion.65
  24.5 2.8 %fusion.45 = (bf16[512,4,128,1]{2,1,0,3:T(4,128)(2,1)S(1)}, bf16[512,4,128,1]{2,1,0,3:T(4,128)(2,1)S(1)}, bf16[512,4,128,1]{2,1,0,3:T(4,128)(2,1)S(1)}) fusion(bf16[3,1,512,4,128]{4,3,2,1,0:T(4,128)(2,1)S(1)} %copy-done, bf16[512]{0:T(512)(128)(2,1)S(1)} %get-tuple-element.26, bf16[4,128]{1,0:T(4,128)(2,1)S(1)} %get-tuple-element.20, ...), kind=kLoop, calls=%fused_computation.40 | loop fusion | flops 1572864 | bytes 3151872 | tf_op jit(solution)/shard_map/mul | solution.py:42
  27.5 0.2 copy_dynamic-update-slice_fusion.11
  27.7 0.7 fusion.77
  28.4 1.2 copy_dynamic-update-slice_fusion.10
  29.6 1.1 copy_dynamic-update-slice_fusion.9
  30.8 7.4 %collective-permute-done.2 = bf16[1,8,128,128]{3,2,1,0:T(8,128)(2,1)S(1)} collective-permute-done((bf16[1,8,128,128]{3,2,1,0:T(8,128)(2,1)}, bf16[1,8,128,128]{3,2,1,0:T(8,128)(2,1)S(1)}, u32[]{:S(2)}, u32[]{:S(2)}) %collective-permute-start.2) | collective-permute-done | bytes 262176 | tf_op jit(solution)/shard_map/ppermute | solution.py:15
  38.4 5.6 %convert_bitcast_fusion.2 = bf16[8,4,512,128]{3,0,1,2:T(8,128)(2,1)} fusion(bf16[8,512,128]{2,0,1:T(8,128)(2,1)S(1)} %copy_dynamic-update-slice_fusion.8, f32[3,4,8,8]{3,2,1,0:T(8,128)} %param.9), kind=kOutput, calls=%fused_computation.11 | convolution fusion | flops 203423744 | bytes 5259264 | tf_op jit(solution)/shard_map/sdc,bcik->bdsik/dot_general | solution.py:44
  44.0 4.4 %fusion.15 = bf16[8,4,128,128]{3,2,0,1:T(8,128)(2,1)S(1)} fusion(bf16[8,4,512,128]{3,0,1,2:T(8,128)(2,1)} %convert_bitcast_fusion.2, bf16[512,4,128,1]{2,1,0,3:T(4,128)(2,1)S(1)} %get-tuple-element.3, bf16[1,1,128,4,128]{4,3,2,1,0:T(4,128)(2,1)S(1)} %copy-done.2), kind=kOutput, calls=%fused_computation.21 | convolution fusion | flops 672137216 | bytes 5898240 | tf_op jit(solution)/shard_map/bdsok,ksl->bdsol/dot_general | solution.py:54
  48.4 0.9 fusion.16
  49.4 0.2 copy.71
  49.6 17.1 %all_to_all.15 = bf16[4,1,8,128,128]{4,3,2,1,0:T(8,128)(2,1)S(1)} all-to-all(bf16[4,1,8,128,128]{4,3,2,1,0:T(8,128)(2,1)S(1)} %copy.71), channel_id=1, replica_groups=mesh['section'=4,'sector'=4,'comp'=2] {'sector'}, dimensions={0} | all-to-all | bytes 2097152 | tf_op jit(solution)/shard_map/all_to_all | solution.py:66
  66.7 0.2 reduce_sum.44
  66.9 3.8 %collective-permute-start.4 = (bf16[1,8,128,128]{3,2,1,0:T(8,128)(2,1)S(1)}, bf16[1,8,128,128]{3,2,1,0:T(8,128)(2,1)S(1)}, u32[]{:S(2)}, u32[]{:S(2)}) collective-permute-start(bf16[1,8,128,128]{3,2,1,0:T(8,128)(2,1)S(1)} %bitcast.208), channel_id=1, source_target_pairs={{0,24},{8,0},{16,8},{24,16},{1,25},{9,1},{17,9},{25,17},{2,26},{10... | collective-permute-start | bytes 786440 | tf_op jit(solution)/shard_map/ppermute | solution.py:18
  71.1 6.9 %collective-permute-done.3 = bf16[1,8,128,128]{3,2,1,0:T(8,128)(2,1)S(1)} collective-permute-done((bf16[1,8,128,128]{3,2,1,0:T(8,128)(2,1)S(1)}, bf16[1,8,128,128]{3,2,1,0:T(8,128)(2,1)S(1)}, u32[]{:S(2)}, u32[]{:S(2)}) %collective-permute-start.3) | collective-permute-done | bytes 262176 | tf_op jit(solution)/shard_map/ppermute | solution.py:15
  78.2 2.1 %collective-permute-done.4 = bf16[1,8,128,128]{3,2,1,0:T(8,128)(2,1)S(1)} collective-permute-done((bf16[1,8,128,128]{3,2,1,0:T(8,128)(2,1)S(1)}, bf16[1,8,128,128]{3,2,1,0:T(8,128)(2,1)S(1)}, u32[]{:S(2)}, u32[]{:S(2)}) %collective-permute-start.4) | collective-permute-done | bytes 262176 | tf_op jit(solution)/shard_map/ppermute | solution.py:18
  80.5 7.2 %collective-permute-done.5 = bf16[1,8,128,128]{3,2,1,0:T(8,128)(2,1)S(1)} collective-permute-done((bf16[1,8,128,128]{3,2,1,0:T(8,128)(2,1)S(1)}, bf16[1,8,128,128]{3,2,1,0:T(8,128)(2,1)S(1)}, u32[]{:S(2)}, u32[]{:S(2)}) %collective-permute-start.5) | collective-permute-done | bytes 262176 | tf_op jit(solution)/shard_map/ppermute | solution.py:15
  87.9 4.9 %convert_bitcast_fusion.1 = bf16[8,4,512,128]{3,0,1,2:T(8,128)(2,1)} fusion(bf16[8,512,128]{2,0,1:T(8,128)(2,1)S(1)} %copy_dynamic-update-slice_fusion.4, f32[3,4,8,8]{3,2,1,0:T(8,128)S(1)} %copy-done.3), kind=kOutput, calls=%fused_computation.10 | convolution fusion | flops 203423744 | bytes 5259264 | tf_op jit(solution)/shard_map/sdc,bcik->bdsik/dot_general | solution.py:44
  92.8 4.4 %fusion.17 = bf16[8,4,128,128]{3,2,0,1:T(8,128)(2,1)S(1)} fusion(bf16[8,4,512,128]{3,0,1,2:T(8,128)(2,1)} %convert_bitcast_fusion.1, bf16[512,4,128,1]{2,1,0,3:T(4,128)(2,1)S(1)} %get-tuple-element.4, bf16[1,1,128,4,128]{4,3,2,1,0:T(4,128)(2,1)S(1)} %copy-done.1), kind=kOutput, calls=%fused_computation.23 | convolution fusion | flops 672137216 | bytes 5898240 | tf_op jit(solution)/shard_map/bdsok,ksl->bdsol/dot_general | solution.py:54
  97.2 0.9 fusion.18
  98.1 0.2 copy.81
  98.4 16.9 %all_to_all.16 = bf16[4,1,8,128,128]{4,3,2,1,0:T(8,128)(2,1)S(1)} all-to-all(bf16[4,1,8,128,128]{4,3,2,1,0:T(8,128)(2,1)S(1)} %copy.81), channel_id=1, replica_groups=mesh['section'=4,'sector'=4,'comp'=2] {'sector'}, dimensions={0} | all-to-all | bytes 2097152 | tf_op jit(solution)/shard_map/all_to_all | solution.py:66
  115.2 0.2 reduce_sum.46
  115.5 3.8 %collective-permute-start.7 = (bf16[1,8,128,128]{3,2,1,0:T(8,128)(2,1)S(1)}, bf16[1,8,128,128]{3,2,1,0:T(8,128)(2,1)S(1)}, u32[]{:S(2)}, u32[]{:S(2)}) collective-permute-start(bf16[1,8,128,128]{3,2,1,0:T(8,128)(2,1)S(1)} %bitcast.211), channel_id=1, source_target_pairs={{0,24},{8,0},{16,8},{24,16},{1,25},{9,1},{17,9},{25,17},{2,26},{10... | collective-permute-start | bytes 786440 | tf_op jit(solution)/shard_map/ppermute | solution.py:18
  119.7 6.9 %collective-permute-done.6 = bf16[1,8,128,128]{3,2,1,0:T(8,128)(2,1)S(1)} collective-permute-done((bf16[1,8,128,128]{3,2,1,0:T(8,128)(2,1)S(1)}, bf16[1,8,128,128]{3,2,1,0:T(8,128)(2,1)S(1)}, u32[]{:S(2)}, u32[]{:S(2)}) %collective-permute-start.6) | collective-permute-done | bytes 262176 | tf_op jit(solution)/shard_map/ppermute | solution.py:15
  126.7 2.1 %collective-permute-done.7 = bf16[1,8,128,128]{3,2,1,0:T(8,128)(2,1)S(1)} collective-permute-done((bf16[1,8,128,128]{3,2,1,0:T(8,128)(2,1)S(1)}, bf16[1,8,128,128]{3,2,1,0:T(8,128)(2,1)S(1)}, u32[]{:S(2)}, u32[]{:S(2)}) %collective-permute-start.7) | collective-permute-done | bytes 262176 | tf_op jit(solution)/shard_map/ppermute | solution.py:18
  129.1 7.2 %collective-permute-done.8 = bf16[1,8,128,128]{3,2,1,0:T(8,128)(2,1)S(1)} collective-permute-done((bf16[1,8,128,128]{3,2,1,0:T(8,128)(2,1)S(1)}, bf16[1,8,128,128]{3,2,1,0:T(8,128)(2,1)S(1)}, u32[]{:S(2)}, u32[]{:S(2)}) %collective-permute-start.8) | collective-permute-done | bytes 262176 | tf_op jit(solution)/shard_map/ppermute | solution.py:15
  136.4 4.9 %convert_bitcast_fusion = bf16[8,4,512,128]{3,0,1,2:T(8,128)(2,1)} fusion(bf16[8,512,128]{2,0,1:T(8,128)(2,1)S(1)} %copy_dynamic-update-slice_fusion, f32[3,4,8,8]{3,2,1,0:T(8,128)S(1)} %copy-done.3), kind=kOutput, calls=%fused_computation.9 | convolution fusion | flops 203423744 | bytes 5259264 | tf_op jit(solution)/shard_map/sdc,bcik->bdsik/dot_general | solution.py:44
  141.3 4.4 %fusion.19 = bf16[8,4,128,128]{3,2,0,1:T(8,128)(2,1)S(1)} fusion(bf16[8,4,512,128]{3,0,1,2:T(8,128)(2,1)} %convert_bitcast_fusion, bf16[512,4,128,1]{2,1,0,3:T(4,128)(2,1)S(1)} %get-tuple-element.2, bf16[1,1,128,4,128]{4,3,2,1,0:T(4,128)(2,1)S(1)} %get-tuple-element.5), kind=kOutput, calls=%fused_computation.25 | convolution fusion | flops 672137216 | bytes 5898240 | tf_op jit(solution)/shard_map/bdsok,ksl->bdsol/dot_general | solution.py:54
  145.8 0.9 fusion.20
  146.7 0.2 copy.91
  146.9 16.9 %all_to_all.17 = bf16[4,1,8,128,128]{4,3,2,1,0:T(8,128)(2,1)S(1)} all-to-all(bf16[4,1,8,128,128]{4,3,2,1,0:T(8,128)(2,1)S(1)} %copy.91), channel_id=1, replica_groups=mesh['section'=4,'sector'=4,'comp'=2] {'sector'}, dimensions={0} | all-to-all | bytes 2097152 | tf_op jit(solution)/shard_map/all_to_all | solution.py:66
  163.8 0.9 reduce_sum.48
  164.7 1.9 %maximum_bitcast_fusion = bf16[3,1,8,1,128,128]{5,4,3,2,1,0:T(8,128)(2,1)} fusion(bf16[1,1,8,128,128]{4,3,2,1,0:T(8,128)(2,1)} %bitcast.213, bf16[1,1,8,128,128]{4,3,2,1,0:T(8,128)(2,1)S(1)} %bitcast.212, bf16[1,1,8,128,128]{4,3,2,1,0:T(8,128)(2,1)S(1)} %bitcast.209), kind=kLoop, calls=%fused_computation.36 | loop fusion | flops 786432 | bytes 1572864 | tf_op jit(solution)/shard_map/broadcast_in_dim | solution.py:70
  166.7 7.1 %reduce-scatter.2.cloned.1.call-done = bf16[4,128,128]{2,1,0:T(8,128)(2,1)} async-done(((bf16[8,128,128]{2,1,0:T(8,128)(2,1)}), bf16[4,128,128]{2,1,0:T(8,128)(2,1)}) %reduce-scatter.2.cloned.1.call-update) | async-done | bytes 131088 | tf_op jit(solution)/shard_map/reduce_scatter | solution.py:72
  (33 shorter events, 2.5 us)
Async XLA Ops:
  7.2 17.3 %copy-start = (bf16[3,1,512,4,128]{4,3,2,1,0:T(4,128)(2,1)S(1)}, bf16[3,1,512,4,128]{4,3,2,1,0:T(4,128)(2,1)}, u32[]{:S(2)}) copy-start(bf16[3,1,512,4,128]{4,3,2,1,0:T(4,128)(2,1)} %param.7) | copy-start | bytes 4718596
  7.2 166.6 %reduce-scatter.2.cloned.1.call-start = ((), (), s32[]{:S(2)}) async-start(), calls=%async_computation.4 | async-start | bytes 393216 | tf_op jit(solution)/shard_map/reduce_scatter | solution.py:72
  11.1 17.3 %collective-permute-start = (bf16[1,8,128,128]{3,2,1,0:T(8,128)(2,1)}, bf16[1,8,128,128]{3,2,1,0:T(8,128)(2,1)}, u32[]{:S(2)}, u32[]{:S(2)}) collective-permute-start(bf16[1,8,128,128]{3,2,1,0:T(8,128)(2,1)} %bitcast_multiply_fusion.3), channel_id=1, source_target_pairs={{0,8},{8,16},{16,24},{24,0},{1,9},{9,17},{17,25},{25,1},{2,10},{10... | collective-permute-start | bytes 786440 | tf_op jit(solution)/shard_map/ppermute | solution.py:15
  14.1 15.5 %collective-permute-start.1 = (bf16[1,8,128,128]{3,2,1,0:T(8,128)(2,1)}, bf16[1,8,128,128]{3,2,1,0:T(8,128)(2,1)}, u32[]{:S(2)}, u32[]{:S(2)}) collective-permute-start(bf16[1,8,128,128]{3,2,1,0:T(8,128)(2,1)} %bitcast_multiply_fusion.3), channel_id=1, source_target_pairs={{0,24},{8,0},{16,8},{24,16},{1,25},{9,1},{17,9},{25,17},{2,26},{10... | collective-permute-start | bytes 786440 | tf_op jit(solution)/shard_map/ppermute | solution.py:18
  27.3 16.7 %copy-start.2 = (bf16[1,1,128,4,128]{4,3,2,1,0:T(4,128)(2,1)S(1)}, bf16[1,1,128,4,128]{4,3,2,1,0:T(4,128)(2,1)}, u32[]{:S(2)}) copy-start(bf16[1,1,128,4,128]{4,3,2,1,0:T(4,128)(2,1)} %get-tuple-element.7) | copy-start | bytes 393220
  28.4 9.8 %collective-permute-start.2 = (bf16[1,8,128,128]{3,2,1,0:T(8,128)(2,1)}, bf16[1,8,128,128]{3,2,1,0:T(8,128)(2,1)S(1)}, u32[]{:S(2)}, u32[]{:S(2)}) collective-permute-start(bf16[1,8,128,128]{3,2,1,0:T(8,128)(2,1)} %collective-permute-done), channel_id=1, source_target_pairs={{0,8},{8,16},{16,24},{24,0},{1,9},{9,17},{17,25},{25,1},{2,10},{10... | collective-permute-start | bytes 786440 | tf_op jit(solution)/shard_map/ppermute | solution.py:15
  49.3 38.5 %copy-start.3 = (f32[3,4,8,8]{3,2,1,0:T(8,128)S(1)}, f32[3,4,8,8]{3,2,1,0:T(8,128)}, u32[]{:S(2)}) copy-start(f32[3,4,8,8]{3,2,1,0:T(8,128)} %param.9) | copy-start | bytes 9220
  66.9 25.9 %copy-start.1 = (bf16[1,1,128,4,128]{4,3,2,1,0:T(4,128)(2,1)S(1)}, bf16[1,1,128,4,128]{4,3,2,1,0:T(4,128)(2,1)}, u32[]{:S(2)}) copy-start(bf16[1,1,128,4,128]{4,3,2,1,0:T(4,128)(2,1)} %get-tuple-element.6) | copy-start | bytes 393220
  66.9 11.1 %collective-permute-start.3 = (bf16[1,8,128,128]{3,2,1,0:T(8,128)(2,1)S(1)}, bf16[1,8,128,128]{3,2,1,0:T(8,128)(2,1)S(1)}, u32[]{:S(2)}, u32[]{:S(2)}) collective-permute-start(bf16[1,8,128,128]{3,2,1,0:T(8,128)(2,1)S(1)} %bitcast.207), channel_id=1, source_target_pairs={{0,8},{8,16},{16,24},{24,0},{1,9},{9,17},{17,25},{25,1},{2,10},{10... | collective-permute-start | bytes 786440 | tf_op jit(solution)/shard_map/ppermute | solution.py:15
  66.9 13.4 %collective-permute-start.4 = (bf16[1,8,128,128]{3,2,1,0:T(8,128)(2,1)S(1)}, bf16[1,8,128,128]{3,2,1,0:T(8,128)(2,1)S(1)}, u32[]{:S(2)}, u32[]{:S(2)}) collective-permute-start(bf16[1,8,128,128]{3,2,1,0:T(8,128)(2,1)S(1)} %bitcast.208), channel_id=1, source_target_pairs={{0,24},{8,0},{16,8},{24,16},{1,25},{9,1},{17,9},{25,17},{2,26},{10... | collective-permute-start | bytes 786440 | tf_op jit(solution)/shard_map/ppermute | solution.py:18
  78.0 9.7 %collective-permute-start.5 = (bf16[1,8,128,128]{3,2,1,0:T(8,128)(2,1)S(1)}, bf16[1,8,128,128]{3,2,1,0:T(8,128)(2,1)S(1)}, u32[]{:S(2)}, u32[]{:S(2)}) collective-permute-start(bf16[1,8,128,128]{3,2,1,0:T(8,128)(2,1)S(1)} %collective-permute-done.3), channel_id=1, source_target_pairs={{0,8},{8,16},{16,24},{24,0},{1,9},{9,17},{17,25},{25,1},{2,10},{10... | collective-permute-start | bytes 786440 | tf_op jit(solution)/shard_map/ppermute | solution.py:15
  115.4 11.1 %collective-permute-start.6 = (bf16[1,8,128,128]{3,2,1,0:T(8,128)(2,1)S(1)}, bf16[1,8,128,128]{3,2,1,0:T(8,128)(2,1)S(1)}, u32[]{:S(2)}, u32[]{:S(2)}) collective-permute-start(bf16[1,8,128,128]{3,2,1,0:T(8,128)(2,1)S(1)} %bitcast.210), channel_id=1, source_target_pairs={{0,8},{8,16},{16,24},{24,0},{1,9},{9,17},{17,25},{25,1},{2,10},{10... | collective-permute-start | bytes 786440 | tf_op jit(solution)/shard_map/ppermute | solution.py:15
  115.5 13.4 %collective-permute-start.7 = (bf16[1,8,128,128]{3,2,1,0:T(8,128)(2,1)S(1)}, bf16[1,8,128,128]{3,2,1,0:T(8,128)(2,1)S(1)}, u32[]{:S(2)}, u32[]{:S(2)}) collective-permute-start(bf16[1,8,128,128]{3,2,1,0:T(8,128)(2,1)S(1)} %bitcast.211), channel_id=1, source_target_pairs={{0,24},{8,0},{16,8},{24,16},{1,25},{9,1},{17,9},{25,17},{2,26},{10... | collective-permute-start | bytes 786440 | tf_op jit(solution)/shard_map/ppermute | solution.py:18
  126.5 9.7 %collective-permute-start.8 = (bf16[1,8,128,128]{3,2,1,0:T(8,128)(2,1)S(1)}, bf16[1,8,128,128]{3,2,1,0:T(8,128)(2,1)S(1)}, u32[]{:S(2)}, u32[]{:S(2)}) collective-permute-start(bf16[1,8,128,128]{3,2,1,0:T(8,128)(2,1)S(1)} %collective-permute-done.6), channel_id=1, source_target_pairs={{0,8},{8,16},{16,24},{24,0},{1,9},{9,17},{17,25},{25,1},{2,10},{10... | collective-permute-start | bytes 786440 | tf_op jit(solution)/shard_map/ppermute | solution.py:15
Sparse Core Ops, SparseCore 0:
  164.9 8.8 reduce-scatter.1
